TPU v7x, 256 devices: a whole 4x4x8 slice. The times are simulated.
256 devices in a mesh: col: 64 (over y, z, core), lev: 4 (over x).
Axes of the slice: x: 4, y: 4, z: 8, core: 2. Of those that a mesh axis runs over, the one named last changes fastest.
Arguments:
- state: float32 [20, 80, 65536], P('lev', None, 'col'), may hold values from -6 to 6
- obs_col: int32 [2, 24576], replicated, may hold values from 0 to 65532, as said below
- obs_count: int32 [2, 64], P(None, 'col'), may hold values from 192 to 384, as said below
- obs_value: float32 [2, 24576], P(None, 'col'), may hold values from -7.5 to 7.5
- obs_var: float32 [2, 24576], P(None, 'col'), may hold values from 0.2 to 2
- horiz_weight: float32 [2, 4, 24576], P(None, None, 'col'), may hold values from 0.1 to 1
- vert_weight: float32 [2, 20, 24576], P(None, 'lev', 'col'), may hold values from 0.05 to 0.5
Outputs:
- analysis: float32 [20, 80, 65536], P('lev', None, 'col')
Inputs may be any that keep to these rules, and one draw needn't show every extreme that they name: Slot s belongs to column block s div 384; its 4 stencil columns obs_col[b, s] to obs_col[b, s] + 3 all lie in that block. `obs_count`: in every batch some column block uses all 384 of its slots.
All inputs are finite; a program needn't handle non-finite values.
Results may differ from a plain program's by a relative error of at most 0.0003.
Values sent between devices are 32-bit elements; how exact they have to be, the bound alone decides.
A program may use at most 64 MiB of HBM per device.

v0:
```python
import jax
import jax.numpy as jnp
from jax import lax
from jax.sharding import PartitionSpec as P

STENCIL = 4


epsilon = 1e-06


def with_halo(block, sides, width):
    for axis, dim in sides:
        count = lax.axis_size(axis)
        forward = [(i, i + 1) for i in range(count - 1)]
        forward.append((count - 1, 0))
        backward = [(target, source) for source, target in forward]
        low = lax.ppermute(
            lax.slice_in_dim(block, block.shape[dim] - width, None, axis=dim), axis, forward
        )
        high = lax.ppermute(lax.slice_in_dim(block, 0, width, axis=dim), axis, backward)
        block = jnp.concatenate([low, block, high], axis=dim)
    return block


def gc_taper(distance, half_width):
    ratio = distance / half_width
    near_part = (((-0.25 * ratio + 0.5) * ratio + 0.625) * ratio - 5.0 / 3.0) * ratio * ratio + 1.0
    ratio_safe = jnp.maximum(ratio, 1.0)
    far_part = (
        (
            (((ratio_safe / 12.0 - 0.5) * ratio_safe + 0.625) * ratio_safe + 5.0 / 3.0) * ratio_safe
            - 5.0
        )
        * ratio_safe
        + 4.0
        - 2.0 / (3.0 * ratio_safe)
    )
    return jnp.where(ratio <= 1.0, near_part, jnp.where(ratio < 2.0, far_part, 0.0 * ratio))


def cycle_taper(obs_cols, columns, cycle_len, reach):
    gap = jnp.mod(obs_cols[:, None] - columns[None, :], cycle_len)
    distance = jnp.minimum(gap, cycle_len - gap).astype(jnp.float32)
    return gc_taper(distance, reach / 2.0)


def increments(obs_anom, innovation, prior_var, noise, inflation, members):
    inflated_var = inflation * prior_var
    mean_shift = inflated_var * innovation / (inflated_var + noise)
    shrink = jnp.sqrt(noise / (inflated_var + noise)) - 1.0
    obs_shift = mean_shift[None, :] + shrink[None, :] * jnp.sqrt(inflation) * obs_anom
    regress = obs_anom / ((members - 1) * (prior_var + epsilon))[None, :]
    return (obs_shift, regress)


def global_totals(misfit_part, expected_part):
    return lax.psum((misfit_part, expected_part), "col")


def shards(state, obs_col, obs_count, obs_value, obs_var, horiz_weight, vert_weight):
    lev_dev, members, col_dev = state.shape
    batches, slots = obs_col.shape
    cap = obs_value.shape[1]
    blocks = lax.axis_size("col")
    cycle_len = col_dev * blocks
    reach = col_dev // 2
    my_block = lax.axis_index("col")
    first_col = my_block * col_dev
    columns = first_col + jnp.arange(col_dev, dtype=jnp.int32)
    near_slots = jnp.mod((my_block - 1) * cap + jnp.arange(3 * cap, dtype=jnp.int32), slots)
    current = state
    for which_batch in range(batches):
        obs_cols = obs_col[which_batch]
        own_start = lax.dynamic_slice_in_dim(obs_cols, my_block * cap, cap) - first_col
        stencil = own_start[None, :] + jnp.arange(STENCIL, dtype=jnp.int32)[:, None]
        picked = jnp.take(current, stencil, axis=2)
        partial_value = jnp.einsum(
            "lmks,ks,ls->ms",
            picked,
            horiz_weight[which_batch],
            vert_weight[which_batch],
            precision=lax.Precision.HIGHEST,
        )
        obs_prior = lax.psum(partial_value, "lev")
        in_use = (jnp.arange(cap, dtype=jnp.int32) < obs_count[which_batch, 0]).astype(jnp.float32)
        obs_mean = jnp.mean(obs_prior, axis=0)
        deviation = obs_prior - obs_mean[None, :]
        prior_var = jnp.sum(deviation * deviation, axis=0) / (members - 1)
        obs_anom = deviation * in_use[None, :]
        innovation = (obs_value[which_batch] - obs_mean) * in_use
        noise = obs_var[which_batch]
        misfit_part = jnp.sum(innovation * innovation)
        expected_part = jnp.sum(in_use * (prior_var + noise))
        misfit, expected = global_totals(misfit_part, expected_part)
        inflation = misfit / expected
        obs_shift, regress = increments(obs_anom, innovation, prior_var, noise, inflation, members)
        packet = jnp.concatenate([obs_shift, regress], axis=0)
        nearby = with_halo(packet, (("col", 1),), cap)
        near_shift = nearby[:members]
        near_regress = nearby[members:]
        near_cols = jnp.take(obs_cols, near_slots)
        loc_weight = cycle_taper(near_cols, columns, cycle_len, reach)
        centre = jnp.mean(current, axis=1, keepdims=True)
        spread = current - centre
        inflated = centre + jnp.sqrt(inflation) * spread

        def one_level(pair):
            level_spread, level_inflated = pair
            coefs = lax.dot_general(
                near_regress,
                level_spread,
                (((0,), (0,)), ((), ())),
                precision=lax.Precision.HIGHEST,
            )
            return level_inflated + jnp.dot(
                near_shift, loc_weight * coefs, precision=lax.Precision.HIGHEST
            )

        current = lax.map(one_level, (spread, inflated))
    return current


def solution(mesh):
    placed = (
        P("lev", None, "col"),
        P(),
        P(None, "col"),
        P(None, "col"),
        P(None, "col"),
        P(None, None, "col"),
        P(None, "lev", "col"),
    )
    return jax.shard_map(
        shards, mesh=mesh, in_specs=placed, out_specs=P("lev", None, "col"), check_vma=False
    )
```

profile of v0, /device:TPU:1, one launch (start us, length us, event | category | flops | bytes accessed | tf_op | source)
XLA Modules:
  0.0 615.6 jit_solution(10672683495324575827)
XLA Ops:
  6.5 1.2 fusion.185
  7.9 3.8 copy.27
  11.8 0.3 copy.46
  12.1 6.7 %gather_fusion = f32[1536,5,80]{2,1,0:T(8,128)} fusion(f32[5,80,1024]{1,0,2:T(8,128)} %copy.27, s32[2048]{0:T(1024)S(1)} %pad_clamp_fusion.2), kind=kCustom, calls=%fused_computation.clone | custom fusion | bytes 4921344 | tf_op jit(solution)/shard_map/jit(_take)/gather | solution.py:77
  18.8 9.1 %fusion.171 = f32[384,80]{1,0:T(8,128)S(1)} fusion(f32[4,384,5,80]{3,2,1,0:T(8,128)} %bitcast.140, f32[384,4,5]{2,0,1:T(8,128)S(1)} %copy.46, pred[4,384]{1,0:T(4,128)(4,1)S(1)} %compare_and_fusion.2), kind=kLoop, calls=%fused_computation.181 | loop fusion | flops 1812480 | bytes 2612736
  27.8 0.8 copy.36
  28.7 0.6 fusion.187
  29.3 0.6 fusion.176
  29.9 0.2 reduce_sum.90
  30.1 6.5 %gather_fusion.1 = s32[1152]{0:T(1024)S(1)} fusion(s32[24576]{0:T(1024)S(1)} %bitcast.139, s32[2048]{0:T(1024)S(1)} %pad_clamp_fusion.1), kind=kCustom, calls=%fused_computation.1.clone | custom fusion | bytes 13824 | tf_op jit(solution)/shard_map/jit(_take)/gather | solution.py:102
  36.6 6.5 %gather_fusion.3 = s32[1152]{0:T(1024)S(1)} fusion(s32[24576]{0:T(1024)S(1)} %bitcast.138, s32[2048]{0:T(1024)S(1)} %pad_clamp_fusion.1), kind=kCustom, calls=%fused_computation.3.clone | custom fusion | bytes 13824 | tf_op jit(solution)/shard_map/jit(_take)/gather | solution.py:102
  43.1 0.6 fusion.175
  43.7 0.3 copy.47
  44.0 32.7 %all-reduce.5.cloned.1.call-done = f32[80,384]{1,0:T(8,128)} async-done(((f32[80,384]{1,0:T(8,128)}), f32[80,384]{1,0:T(8,128)}) %all-reduce.5.cloned.1.call-update) | async-done | bytes 122896 | tf_op jit(solution)/shard_map/psum | solution.py:85
  76.8 0.9 reduce_sum.91
  77.7 1.2 multiply_reduce_fusion.3
  78.8 0.9 multiply_reduce_fusion.1
  79.8 1.2 select_reduce_fusion.1
  81.0 127.4 %all-reduce.1 = (f32[]{:T(128)}, f32[]{:T(128)}) all-reduce(f32[]{:T(128)} %get-tuple-element.189, f32[]{:T(128)} %select_reduce_fusion.1), channel_id=1, replica_groups=mesh['col'=64,'lev'=4] {'col'}, use_global_device_ids=true, to_apply=%region_4.6 | all-reduce | flops 2 | bytes 16 | tf_op jit(solution)/shard_map/psum | solution.py:58
  209.8 0.6 fusion.182
  210.4 0.9 multiply_add_fusion.3
  211.5 3.2 collective-permute-start.1
  214.7 2.1 broadcast_subtract_fusion.1
  216.8 0.5 collective-permute-done.1
  217.5 0.2 broadcast.220.clone
  217.6 92.6 %while.22 = (s32[]{:T(128)}, f32[5,80,1024]{2,1,0:T(8,128)S(1)}, f32[5,80,1024]{2,1,0:T(8,128)}, f32[5,80,1024]{2,1,0:T(8,128)}, f32[80,1152]{1,0:T(8,128)S(1)},...) while((s32[]{:T(128)}, f32[5,80,1024]{2,1,0:T(8,128)S(1)}, ...), condition=%wide.region_9.12_spmd.clone, body=%wide.region_8.11_spmd.clone.sunk | while | flops 2318090240 | bytes 11170401 | solution.py:120
  217.7 5.0 fusion.208
  222.7 13.4 %fusion.209 = f32[5,80,1024]{2,1,0:T(8,128)S(1)} fusion(f32[5,80,1024]{2,1,0:T(8,128)S(1)} %get-tuple-element.307, s32[]{:T(128)} %get-tuple-element.306, f32[80,1152]{1,0:T(8,128)S(1)} %get-tuple-element.320, f32[1024,1152]{1,0:T(8,128)S(1)} %fusion.208, s32[1024]{0:T(1024)S(1)} %get-tuple-element.321, s32[1152]{0:T(1024)S(1)} %get-tuple-element.322, ...), kind=kOutput, calls=%fused_computation.70.clone.1 | convolution fusion | flops 1185628160 | bytes 5754884 | tf_op jit(solution)/shard_map/while/body/eval_jaxpr/dot_general | solution.py:116
  236.2 5.0 fusion.208
  241.2 13.4 %fusion.209 = f32[5,80,1024]{2,1,0:T(8,128)S(1)} fusion(f32[5,80,1024]{2,1,0:T(8,128)S(1)} %get-tuple-element.307, s32[]{:T(128)} %get-tuple-element.306, f32[80,1152]{1,0:T(8,128)S(1)} %get-tuple-element.320, f32[1024,1152]{1,0:T(8,128)S(1)} %fusion.208, s32[1024]{0:T(1024)S(1)} %get-tuple-element.321, s32[1152]{0:T(1024)S(1)} %get-tuple-element.322, ...), kind=kOutput, calls=%fused_computation.70.clone.1 | convolution fusion | flops 1185628160 | bytes 5754884 | tf_op jit(solution)/shard_map/while/body/eval_jaxpr/dot_general | solution.py:116
  254.7 5.0 fusion.208
  259.8 13.4 %fusion.209 = f32[5,80,1024]{2,1,0:T(8,128)S(1)} fusion(f32[5,80,1024]{2,1,0:T(8,128)S(1)} %get-tuple-element.307, s32[]{:T(128)} %get-tuple-element.306, f32[80,1152]{1,0:T(8,128)S(1)} %get-tuple-element.320, f32[1024,1152]{1,0:T(8,128)S(1)} %fusion.208, s32[1024]{0:T(1024)S(1)} %get-tuple-element.321, s32[1152]{0:T(1024)S(1)} %get-tuple-element.322, ...), kind=kOutput, calls=%fused_computation.70.clone.1 | convolution fusion | flops 1185628160 | bytes 5754884 | tf_op jit(solution)/shard_map/while/body/eval_jaxpr/dot_general | solution.py:116
  273.2 5.0 fusion.208
  278.3 13.4 %fusion.209 = f32[5,80,1024]{2,1,0:T(8,128)S(1)} fusion(f32[5,80,1024]{2,1,0:T(8,128)S(1)} %get-tuple-element.307, s32[]{:T(128)} %get-tuple-element.306, f32[80,1152]{1,0:T(8,128)S(1)} %get-tuple-element.320, f32[1024,1152]{1,0:T(8,128)S(1)} %fusion.208, s32[1024]{0:T(1024)S(1)} %get-tuple-element.321, s32[1152]{0:T(1024)S(1)} %get-tuple-element.322, ...), kind=kOutput, calls=%fused_computation.70.clone.1 | convolution fusion | flops 1185628160 | bytes 5754884 | tf_op jit(solution)/shard_map/while/body/eval_jaxpr/dot_general | solution.py:116
  291.8 5.0 fusion.208
  296.8 13.4 %fusion.209 = f32[5,80,1024]{2,1,0:T(8,128)S(1)} fusion(f32[5,80,1024]{2,1,0:T(8,128)S(1)} %get-tuple-element.307, s32[]{:T(128)} %get-tuple-element.306, f32[80,1152]{1,0:T(8,128)S(1)} %get-tuple-element.320, f32[1024,1152]{1,0:T(8,128)S(1)} %fusion.208, s32[1024]{0:T(1024)S(1)} %get-tuple-element.321, s32[1152]{0:T(1024)S(1)} %get-tuple-element.322, ...), kind=kOutput, calls=%fused_computation.70.clone.1 | convolution fusion | flops 1185628160 | bytes 5754884 | tf_op jit(solution)/shard_map/while/body/eval_jaxpr/dot_general | solution.py:116
  310.3 2.8 copy.29
  313.1 6.7 %gather_fusion.2 = f32[1536,5,80]{2,1,0:T(8,128)} fusion(f32[5,80,1024]{1,0,2:T(8,128)} %copy.29, s32[2048]{0:T(1024)S(1)} %pad_clamp_fusion), kind=kCustom, calls=%fused_computation.2.clone | custom fusion | bytes 4921344 | tf_op jit(solution)/shard_map/jit(_take)/gather | solution.py:77
  319.8 8.9 %fusion.170 = f32[384,80]{1,0:T(8,128)S(1)} fusion(f32[4,384,5,80]{3,2,1,0:T(8,128)} %bitcast.141, f32[384,4,5]{2,0,1:T(8,128)S(1)} %copy.47, pred[4,384]{1,0:T(4,128)(4,1)S(1)} %compare_and_fusion.1), kind=kLoop, calls=%fused_computation.179 | loop fusion | flops 1812480 | bytes 2612736
  328.7 0.8 copy.43
  329.5 0.2 reduce_sum.95
  329.7 46.5 %all-reduce.7.cloned.1.call-done = f32[80,384]{1,0:T(8,128)} async-done(((f32[80,384]{1,0:T(8,128)}), f32[80,384]{1,0:T(8,128)}) %all-reduce.7.cloned.1.call-update) | async-done | bytes 122896 | tf_op jit(solution)/shard_map/psum | solution.py:85
  376.2 0.9 reduce_sum.96
  377.1 1.1 broadcast_multiply_fusion.4
  378.2 0.9 multiply_reduce_fusion
  379.2 1.1 select_reduce_fusion
  380.3 127.3 %all-reduce = (f32[]{:T(128)}, f32[]{:T(128)}) all-reduce(f32[]{:T(128)} %get-tuple-element.186, f32[]{:T(128)} %select_reduce_fusion), channel_id=1, replica_groups=mesh['col'=64,'lev'=4] {'col'}, use_global_device_ids=true, to_apply=%region_14.17 | all-reduce | flops 2 | bytes 16 | tf_op jit(solution)/shard_map/psum | solution.py:58
  508.9 0.6 fusion.181
  509.5 0.9 multiply_add_fusion.2
  510.6 3.3 collective-permute-start.3
  513.8 1.7 broadcast_subtract_fusion
  515.5 1.0 collective-permute-done.3
  516.6 1.4 broadcast.220
  518.0 90.8 %while.23 = (s32[]{:T(128)}, f32[5,80,1024]{2,1,0:T(8,128)}, f32[5,80,1024]{2,1,0:T(8,128)}, f32[5,80,1024]{2,1,0:T(8,128)S(1)}, f32[80,1152]{1,0:T(8,128)S(1)},...) while((s32[]{:T(128)}, f32[5,80,1024]{2,1,0:T(8,128)}, ...), condition=%wide.region_19.22_spmd.clone, body=%wide.region_18.21_spmd.clone.sunk | while | flops 2318090240 | bytes 11166817 | solution.py:120
  518.0 4.1 fusion.214
  522.1 14.1 %fusion.215 = f32[5,80,1024]{2,1,0:T(8,128)} fusion(f32[5,80,1024]{2,1,0:T(8,128)} %get-tuple-element.334, s32[]{:T(128)} %get-tuple-element.333, f32[80,1152]{1,0:T(8,128)S(1)} %get-tuple-element.347, f32[1024,1152]{1,0:T(8,128)S(1)} %fusion.214, s32[1024]{0:T(1024)S(1)} %get-tuple-element.348, s32[1152]{0:T(1024)S(1)} %get-tuple-element.349, ...), kind=kOutput, calls=%fused_computation.156.clone.1 | convolution fusion | flops 1185628160 | bytes 5751808 | tf_op jit(solution)/shard_map/while/body/eval_jaxpr/dot_general | solution.py:116
  536.1 4.1 fusion.214
  540.2 14.1 %fusion.215 = f32[5,80,1024]{2,1,0:T(8,128)} fusion(f32[5,80,1024]{2,1,0:T(8,128)} %get-tuple-element.334, s32[]{:T(128)} %get-tuple-element.333, f32[80,1152]{1,0:T(8,128)S(1)} %get-tuple-element.347, f32[1024,1152]{1,0:T(8,128)S(1)} %fusion.214, s32[1024]{0:T(1024)S(1)} %get-tuple-element.348, s32[1152]{0:T(1024)S(1)} %get-tuple-element.349, ...), kind=kOutput, calls=%fused_computation.156.clone.1 | convolution fusion | flops 1185628160 | bytes 5751808 | tf_op jit(solution)/shard_map/while/body/eval_jaxpr/dot_general | solution.py:116
  554.3 4.1 fusion.214
  558.4 14.1 %fusion.215 = f32[5,80,1024]{2,1,0:T(8,128)} fusion(f32[5,80,1024]{2,1,0:T(8,128)} %get-tuple-element.334, s32[]{:T(128)} %get-tuple-element.333, f32[80,1152]{1,0:T(8,128)S(1)} %get-tuple-element.347, f32[1024,1152]{1,0:T(8,128)S(1)} %fusion.214, s32[1024]{0:T(1024)S(1)} %get-tuple-element.348, s32[1152]{0:T(1024)S(1)} %get-tuple-element.349, ...), kind=kOutput, calls=%fused_computation.156.clone.1 | convolution fusion | flops 1185628160 | bytes 5751808 | tf_op jit(solution)/shard_map/while/body/eval_jaxpr/dot_general | solution.py:116
  572.5 4.1 fusion.214
  576.5 14.1 %fusion.215 = f32[5,80,1024]{2,1,0:T(8,128)} fusion(f32[5,80,1024]{2,1,0:T(8,128)} %get-tuple-element.334, s32[]{:T(128)} %get-tuple-element.333, f32[80,1152]{1,0:T(8,128)S(1)} %get-tuple-element.347, f32[1024,1152]{1,0:T(8,128)S(1)} %fusion.214, s32[1024]{0:T(1024)S(1)} %get-tuple-element.348, s32[1152]{0:T(1024)S(1)} %get-tuple-element.349, ...), kind=kOutput, calls=%fused_computation.156.clone.1 | convolution fusion | flops 1185628160 | bytes 5751808 | tf_op jit(solution)/shard_map/while/body/eval_jaxpr/dot_general | solution.py:116
  590.6 4.1 fusion.214
  594.7 14.1 %fusion.215 = f32[5,80,1024]{2,1,0:T(8,128)} fusion(f32[5,80,1024]{2,1,0:T(8,128)} %get-tuple-element.334, s32[]{:T(128)} %get-tuple-element.333, f32[80,1152]{1,0:T(8,128)S(1)} %get-tuple-element.347, f32[1024,1152]{1,0:T(8,128)S(1)} %fusion.214, s32[1024]{0:T(1024)S(1)} %get-tuple-element.348, s32[1152]{0:T(1024)S(1)} %get-tuple-element.349, ...), kind=kOutput, calls=%fused_computation.156.clone.1 | convolution fusion | flops 1185628160 | bytes 5751808 | tf_op jit(solution)/shard_map/while/body/eval_jaxpr/dot_general | solution.py:116
  (50 shorter events, 0.8 us)
Async XLA Ops:
  6.5 5.1 copy-start.1
  6.5 5.2 copy-start.4
  6.5 70.2 %all-reduce.5.cloned.1.call-start = ((), (), s32[]{:S(2)}) async-start(), calls=%async_computation | async-start | bytes 245760 | tf_op jit(solution)/shard_map/psum | solution.py:85
  18.8 10.0 %copy-start.5 = (s32[2,1]{0,1:T(1,128)S(1)}, s32[2,1]{0,1:T(1,128)}, u32[]{:S(2)}) copy-start(s32[2,1]{0,1:T(1,128)} %param.17) | copy-start | bytes 28
  18.8 10.5 %copy-start.2 = (f32[2,384]{1,0:T(2,128)S(1)}, f32[2,384]{1,0:T(2,128)}, u32[]{:S(2)}) copy-start(f32[2,384]{1,0:T(2,128)} %param.18) | copy-start | bytes 9220
  18.8 11.1 %copy-start = (f32[5,80,1024]{2,1,0:T(8,128)S(1)}, f32[5,80,1024]{2,1,0:T(8,128)}, u32[]{:S(2)}) copy-start(f32[5,80,1024]{2,1,0:T(8,128)} %param.15) | copy-start | bytes 4915204
  28.6 347.5 %all-reduce.7.cloned.1.call-start = ((), (), s32[]{:S(2)}) async-start(), calls=%async_computation.1 | async-start | bytes 245760 | tf_op jit(solution)/shard_map/psum | solution.py:85
  36.6 7.4 %copy-start.3 = (f32[2,384]{1,0:T(2,128)S(1)}, f32[2,384]{1,0:T(2,128)}, u32[]{:S(2)}) copy-start(f32[2,384]{1,0:T(2,128)} %param.19) | copy-start | bytes 9220
  211.4 5.4 collective-permute-start
  211.5 5.9 collective-permute-start.1
  510.5 5.0 collective-permute-start.2
  510.6 5.9 collective-permute-start.3
Sparse Core Ops, SparseCore 0:
  28.7 47.9 all-reduce.4
  329.6 46.4 all-reduce.6
where the time goes:
time: 621 us; the launch traced here: 616 us
  blocking collectives  255 us (41%)
  matrix products  183 us (29%)
  waiting for transfers between devices  80.8 us (13%)
  local copies, waits for them, and re-layouts  38.6 us (6%)
  other arithmetic  35 us (6%)
  between operations  16.5 us (3%)
  starting transfers between devices  6.68 us (1%)
    psum x2, blocking collectives, global_totals(): return lax.psum((misfit_part, expected_part), 'col')  255 us
    dot_general x10, matrix products, one_level(): jnp.dot(near_shift, loc_weight * coefs, precision=lax.Precision.HIGHEST)  138 us
    psum x2, waiting for transfers between devices, shards(): obs_prior = lax.psum(partial_value, 'lev')  79.2 us
    dot_general x10, matrix products, one_level(): lax.dot_general(near_regress, level_spread, (((0,), (0,)), ((), ())), pre...  45.6 us
    unnamed x3, other arithmetic  18 us
    gather x2, local copies, waits for them, and re-layouts, shards(): picked = jnp.take(current, stencil, axis=2)  13.4 us
    gather x2, local copies, waits for them, and re-layouts, shards(): near_cols = jnp.take(obs_cols, near_slots)  13 us
  transfers between devices with their start and end apart: 6, of which 4 were waited for; matrix products, arithmetic and copies ran while one was open for 3% of the time, Pallas kernels for 0%

commit v1 on v0

v1 whole, which is shorter than its diff:
```python
import functools
import jax
import jax.numpy as jnp
from jax import lax
from jax.experimental import pallas as pl
from jax.experimental.pallas import tpu as pltpu
from jax.sharding import PartitionSpec as P

MESH = pl.DeviceIdType.MESH
F32 = jnp.float32
BF16 = jnp.bfloat16

BATCHES = 2
LEV = 5
MEM = 80
COLS = 1024
CAP = 384
QUART = 96
LANES = 128
HALF = 512
NZ = 8
NY = 4
NLEV = 4
EPS = 1e-06


def split(x):
    hi = x.astype(BF16)
    return hi, (x - hi.astype(F32)).astype(BF16)


def pad_quarters(x):
    return [
        (x if q == 0 else pltpu.roll(x, CAP - QUART * q, 1))[:, :LANES]
        for q in range(4)
    ]


def pack_quarters(q0, q1, q2, q3):
    lane = lax.broadcasted_iota(jnp.int32, q0.shape, 1)
    r1 = pltpu.roll(q1, 96, 1)
    r2 = pltpu.roll(q2, 64, 1)
    r3 = pltpu.roll(q3, 32, 1)
    return jnp.concatenate(
        [
            jnp.where(lane < 96, q0, r1),
            jnp.where(lane < 64, r1, r2),
            jnp.where(lane < 32, r2, r3),
        ],
        axis=1,
    )


def taper(dist):
    r = dist * (1.0 / 256.0)
    near = (((-0.25 * r + 0.5) * r + 0.625) * r - 5.0 / 3.0) * (r * r) + 1.0
    t = jnp.maximum(2.0 - r, 0.0)
    t2 = t * t
    rs = jnp.maximum(r, 1.0)
    far = (t2 * t2) * ((rs + 2.0) * rs - 0.5) * pl.reciprocal(12.0 * rs)
    return jnp.where(r <= 1.0, near, far)


def remote(src, dst, send, recv, dev):
    return pltpu.make_async_remote_copy(
        src_ref=src, dst_ref=dst, send_sem=send, recv_sem=recv,
        device_id=dev, device_id_type=MESH,
    )


def kernel(
    state, obs_col, obs_count, obs_value, obs_var, hw, vw, out,
    X, CEN, SPC, XHL, HH, HL, LOC, PT, RT, SC, ZH, ZL, MV, META, PART, RSB, PRI, G1, G2,
    dma_sem, meta_s, meta_r, rs_s, rs_r, ag_s, ag_r, ha_s, ha_r, g1_s, g1_r, g2_s, g2_r,
):
    i = lax.axis_index("col")
    j = lax.axis_index("lev")
    core = lax.rem(i, 2)
    z = lax.rem(i // 2, NZ)
    y = i // (2 * NZ)
    left = lax.rem(i + 63, 64)
    right = lax.rem(i + 1, 64)
    lev_peers = [lax.rem(j + d, NLEV) for d in range(NLEV)]
    g1_peers = [
        {"col": lax.rem(y + dy, NY) * 16 + z * 2 + core, "lev": lax.rem(j + dl, NLEV)}
        for dl in range(NLEV) for dy in range(NY) if dl or dy
    ]
    g2_peers = [
        {"col": y * 16 + lax.rem(z + dz, NZ) * 2 + lax.rem(core + dc, 2), "lev": j}
        for dz in range(NZ) for dc in range(2) if dz or dc
    ]
    g1_me = j * NY + y
    g2_me = z * 2 + core

    barrier = pltpu.get_barrier_semaphore()
    partners = g1_peers + g2_peers + [{"col": left, "lev": j}, {"col": right, "lev": j}]
    for dev in partners:
        pl.semaphore_signal(barrier, inc=1, device_id=dev, device_id_type=MESH)
    load = pltpu.make_async_copy(state, X, dma_sem)
    load.start()

    starts = [obs_col[:, pl.ds(pl.multiple_of(b * CAP, CAP), CAP)] for b in (i, left, right)]
    lane384 = lax.broadcasted_iota(jnp.int32, (1, CAP), 1)
    use = [(lane384 < obs_count[b, 0]).astype(F32) for b in range(BATCHES)]
    META[0] = jnp.concatenate(
        [obs_value[...], obs_var[...], use[0], use[1], jnp.zeros((2, CAP), F32)], axis=0
    )
    MV[...] = jnp.stack(pad_quarters(META[0]))
    rel = [
        (starts[0] - i * COLS).astype(F32),
        (starts[1] - left * COLS - COLS).astype(F32),
        (starts[2] - right * COLS + COLS).astype(F32),
    ]
    PT[...] = jnp.concatenate(rel + [jnp.zeros((LANES - 6, CAP), F32)], axis=0).T

    def build_gather(b):
        lane = lax.broadcasted_iota(jnp.int32, (1, LANES), 1)
        valid = lane < QUART
        st = pad_quarters(starts[0] - i * COLS)
        h4 = pad_quarters(hw[b])
        start = jnp.concatenate([s[b : b + 1] for s in st], axis=1)
        w = jnp.concatenate([jnp.where(valid, h, 0.0) for h in h4], axis=1)

        @pl.loop(0, COLS // 32)
        def _(k):
            rows = pl.ds(pl.multiple_of(k * 32, 32), 32)
            t = lax.broadcasted_iota(jnp.int32, (32, 4 * LANES), 0) + (k * 32 - start)
            m = jnp.zeros((32, 4 * LANES), F32)
            for n in range(4):
                m = jnp.where(t == n, w[n : n + 1], m)
            HH[b, rows, :], HL[b, rows, :] = split(m)

    def build_taper(b):
        for half in range(2):
            for grp in range(2):
                blk = 0 if grp == 0 else 1 + half

                @pl.loop(0, CAP // 32)
                def _(k):
                    rows = pl.ds(pl.multiple_of(k * 32, 32), 32)
                    p = PT[rows, 2 * blk + b : 2 * blk + b + 1]
                    c = (lax.broadcasted_iota(jnp.int32, (32, HALF), 1) + half * HALF).astype(F32)
                    LOC[b, half, grp, rows, :] = taper(jnp.abs(p - c))

    def partial_priors(b):
        @pl.loop(0, LEV)
        def _(l):
            x = X[l]
            hi, lo = split(x)
            XHL[pl.ds(pl.multiple_of(l * MEM, MEM), MEM), :] = hi
            XHL[pl.ds(pl.multiple_of(LEV * MEM + l * MEM, MEM), MEM), :] = lo

        v4 = pad_quarters(vw[b])
        for n in range(2):
            cols = slice(n * 256, n * 256 + 256)
            a = jnp.dot(XHL[...], HH[b, :, cols], preferred_element_type=F32)
            r = jnp.dot(XHL[: LEV * MEM], HL[b, :, cols], preferred_element_type=F32)
            v = jnp.concatenate([v4[2 * n], v4[2 * n + 1]], axis=1)
            total = None
            for l in range(LEV):
                term = a[l * MEM : (l + 1) * MEM] + a[(LEV + l) * MEM : (LEV + l + 1) * MEM]
                term = (term + r[l * MEM : (l + 1) * MEM]) * v[l : l + 1]
                total = term if total is None else total + term
            PART[b, 2 * n] = total[:, :LANES]
            PART[b, 2 * n + 1] = total[:, LANES:]

    def prepare_spread():
        @pl.loop(0, LEV)
        def _(l):
            x = X[l]
            centre = jnp.mean(x, axis=0, keepdims=True)
            CEN[l] = jnp.broadcast_to(centre, (8, COLS))
            hi, lo = split(x - centre)
            SPC[l, 0:MEM] = hi
            SPC[l, MEM : 2 * MEM] = hi
            SPC[l, 2 * MEM : 3 * MEM] = lo
            SPC[l, 3 * MEM :] = jnp.zeros((16, COLS), BF16)

    def stats(prior):
        mean = jnp.sum(prior, axis=0, keepdims=True) / MEM
        dev = prior - mean
        var = jnp.sum(dev * dev, axis=0, keepdims=True) / (MEM - 1)
        return mean, dev, var

    build_gather(0)
    load.wait()
    partial_priors(0)
    pl.semaphore_wait(barrier, len(partners))

    meta_copies = [
        remote(META.at[0], META.at[1], meta_s.at[0], meta_r.at[0], {"col": right, "lev": j}),
        remote(META.at[0], META.at[2], meta_s.at[1], meta_r.at[1], {"col": left, "lev": j}),
    ]
    pending = []

    for b in range(BATCHES):
        copies = []
        for d in (2, 1, 3):
            c = remote(PART.at[b, lev_peers[d]], RSB.at[b, d - 1], rs_s.at[b, d - 1], rs_r.at[b, d - 1],
                       {"col": i, "lev": lev_peers[d]})
            c.start()
            copies.append(c)
        if b == 0:
            for c in meta_copies:
                c.start()
            build_taper(0)
        prepare_spread()
        for c in copies:
            c.wait_recv()
        pending += copies
        prior = PART[b, j] + (RSB[b, 0] + RSB[b, 1] + RSB[b, 2])
        PRI[b, 0, j] = prior

        def forward(q):
            made = [
                remote(PRI.at[b, 0, q], PRI.at[b, 1, q], ha_s.at[b, 0, q], ha_r.at[b, 0, q],
                       {"col": right, "lev": j}),
                remote(PRI.at[b, 0, q], PRI.at[b, 2, q], ha_s.at[b, 1, q], ha_r.at[b, 1, q],
                       {"col": left, "lev": j}),
            ]
            for c in made:
                c.start()
            pending.extend(made)

        gathers = []
        for d in (2, 1, 3):
            c = remote(PRI.at[b, 0, j], PRI.at[b, 0, j], ag_s.at[b, d - 1], ag_r.at[b, d - 1],
                       {"col": i, "lev": lev_peers[d]})
            c.start()
            gathers.append((d, c))
        forward(j)

        mean, dev, var = stats(prior)
        lane = lax.broadcasted_iota(jnp.int32, (1, LANES), 1)
        value = MV[j, b : b + 1]
        noise = MV[j, 2 + b : 3 + b]
        used = jnp.where(lane < QUART, MV[j, 4 + b : 5 + b], 0.0)
        innov = (value - mean) * used
        misfit = jnp.sum(innov * innov, axis=1, keepdims=True)
        expected = jnp.sum(used * (var + noise), axis=1, keepdims=True)
        G1[b, pl.ds(g1_me, 1), :] = jnp.where(lane < 64, misfit, expected)
        for dev_id in g1_peers:
            row = G1.at[b, pl.ds(g1_me, 1)]
            remote(row, row, g1_s.at[b], g1_r.at[b], dev_id).start()
        if b == 0:
            build_gather(1)
        for d, c in gathers:
            c.wait_recv()
            forward(lax.rem(j + NLEV - d, NLEV))
        pending += [c for _, c in gathers]

        all15 = G1.at[b, pl.ds(0, 15)]
        remote(all15, all15, g1_s.at[b], g1_r.at[b], g1_peers[0]).wait()
        G2[b, pl.ds(g2_me, 1), :] = jnp.sum(G1[b], axis=0, keepdims=True)
        for dev_id in g2_peers:
            row = G2.at[b, pl.ds(g2_me, 1)]
            remote(row, row, g2_s.at[b], g2_r.at[b], dev_id).start()

        kept = []

        def regression(blk):
            prior3 = pack_quarters(*[PRI[b, blk, q] for q in range(4)])
            mean, dev, var = stats(prior3)
            used = META[blk, 4 + b : 5 + b]
            anom = dev * used
            innov = (META[blk, b : b + 1] - mean) * used
            kept.append((anom, innov, var))
            regress = anom / ((MEM - 1) * (var + EPS))
            hi = regress.astype(BF16).astype(F32)
            lo = regress - hi
            for t in range(3):
                cut = slice(t * LANES, (t + 1) * LANES)
                tall = jnp.concatenate([hi[:, cut], lo[:, cut], hi[:, cut], jnp.zeros((16, LANES), F32)], axis=0)
                RT[blk, cut, :] = tall.T.astype(BF16)

        def first_product(grp):
            @pl.loop(0, LEV)
            def _(l):
                for c4 in range(4):
                    half, ct = c4 // 2, c4 % 2
                    blk = 0 if grp == 0 else 1 + half
                    cols = slice(c4 * 256, c4 * 256 + 256)
                    coef = jnp.dot(RT[blk], SPC[l, :, cols], preferred_element_type=F32)
                    hi, lo = split(coef * LOC[b, half, grp, :, ct * 256 : ct * 256 + 256])
                    ZH[l, grp * CAP : (grp + 1) * CAP, cols] = hi
                    ZL[l, grp * CAP : (grp + 1) * CAP, cols] = lo

        regression(0)
        first_product(0)
        if b == 0:
            for c in meta_copies:
                c.wait()
            build_taper(1)
        for side in range(2):
            for q in range(4):
                remote(PRI.at[b, 0, q], PRI.at[b, 1 + side, q], ha_s.at[b, side, q], ha_r.at[b, side, q],
                       {"col": right, "lev": j}).wait_recv()
        regression(1)
        regression(2)
        first_product(1)

        all15 = G2.at[b, pl.ds(0, 15)]
        remote(all15, all15, g2_s.at[b], g2_r.at[b], g2_peers[0]).wait()
        sums = jnp.sum(G2[b], axis=0, keepdims=True)
        inflation = sums[:, 0:1] / sums[:, 64:65]
        root = jnp.sqrt(inflation)
        for blk in range(3):
            anom, innov, var = kept[blk]
            noise = META[blk, 2 + b : 3 + b]
            v = inflation * var
            tot = v + noise
            shift = v * innov / tot + ((jnp.sqrt(noise / tot) - 1.0) * root) * anom
            hi, lo = split(shift)
            cut = slice(0, CAP) if blk == 0 else slice(CAP, 2 * CAP)
            for half in ((0, 1) if blk == 0 else (blk - 1,)):
                SC[half, 0:MEM, cut] = hi
                SC[half, MEM : 2 * MEM, cut] = lo

        target = X if b + 1 < BATCHES else out

        @pl.loop(0, LEV)
        def _(l):
            for c4 in range(4):
                half = c4 // 2
                cols = slice(c4 * 256, c4 * 256 + 256)
                a = jnp.dot(SC[half], ZH[l, :, cols], preferred_element_type=F32)
                r = jnp.dot(SC[half, 0:MEM], ZL[l, :, cols], preferred_element_type=F32)
                centre = CEN[l, 0:1, cols]
                base = centre + root * (X[l, :, cols] - centre)
                target[l, :, cols] = base + (a[:MEM] + a[MEM:] + r)

        if b + 1 < BATCHES:
            partial_priors(b + 1)

    for c in pending:
        c.wait_send()


def shards(state, obs_col, obs_count, obs_value, obs_var, horiz_weight, vert_weight):
    vm = pl.BlockSpec(memory_space=pltpu.VMEM)
    dma = pltpu.SemaphoreType.DMA
    return pl.pallas_call(
        kernel,
        name="window",
        out_shape=jax.ShapeDtypeStruct((LEV, MEM, COLS), F32),
        in_specs=[pl.BlockSpec(memory_space=pl.ANY), vm, pl.BlockSpec(memory_space=pltpu.SMEM), vm, vm, vm, vm],
        out_specs=vm,
        scratch_shapes=[
            pltpu.VMEM((LEV, MEM, COLS), F32),
            pltpu.VMEM((LEV, 8, COLS), F32),
            pltpu.VMEM((LEV, 256, COLS), BF16),
            pltpu.VMEM((2 * LEV * MEM, COLS), BF16),
            pltpu.VMEM((BATCHES, COLS, 4 * LANES), BF16),
            pltpu.VMEM((BATCHES, COLS, 4 * LANES), BF16),
            pltpu.VMEM((BATCHES, 2, 2, CAP, HALF), F32),
            pltpu.VMEM((CAP, LANES), F32),
            pltpu.VMEM((3, CAP, 256), BF16),
            pltpu.VMEM((2, 2 * MEM, 2 * CAP), BF16),
            pltpu.VMEM((LEV, 2 * CAP, COLS), BF16),
            pltpu.VMEM((LEV, 2 * CAP, COLS), BF16),
            pltpu.VMEM((4, 8, LANES), F32),
            pltpu.VMEM((3, 8, CAP), F32),
            pltpu.VMEM((BATCHES, 4, MEM, LANES), F32),
            pltpu.VMEM((BATCHES, 3, MEM, LANES), F32),
            pltpu.VMEM((BATCHES, 3, 4, MEM, LANES), F32),
            pltpu.VMEM((BATCHES, 16, LANES), F32),
            pltpu.VMEM((BATCHES, 16, LANES), F32),
            dma,
            dma((2,)), dma((2,)),
            dma((BATCHES, 3)), dma((BATCHES, 3)),
            dma((BATCHES, 3)), dma((BATCHES, 3)),
            dma((BATCHES, 2, 4)), dma((BATCHES, 2, 4)),
            dma((BATCHES,)), dma((BATCHES,)),
            dma((BATCHES,)), dma((BATCHES,)),
        ],
        compiler_params=pltpu.CompilerParams(
            collective_id=0, has_side_effects=True, vmem_limit_bytes=56 * 1024 * 1024
        ),
    )(state, obs_col, obs_count, obs_value, obs_var, horiz_weight, vert_weight)


def solution(mesh):
    placed = (
        P("lev", None, "col"),
        P(),
        P(None, "col"),
        P(None, "col"),
        P(None, "col"),
        P(None, None, "col"),
        P(None, "lev", "col"),
    )
    return jax.shard_map(
        shards, mesh=mesh, in_specs=placed, out_specs=P("lev", None, "col"), check_vma=False
    )
```

time: 621 us -> 65.8 us (0.11)
  blocking collectives: 255 us -> 0 us
  matrix products: 183 us -> 0 us
  waiting for transfers between devices: 80.8 us -> 0 us
  Pallas kernels: 0 us -> 60.1 us
  other arithmetic: 35 us -> 0 us
  local copies, waits for them, and re-layouts: 38.6 us -> 5.42 us
  between operations: 16.5 us -> 0.01 us
  starting transfers between devices: 6.68 us -> 0 us
    psum x2 -> x0, blocking collectives: 255 us -> none  [global_totals(): return lax.psum((misfit_part, expected_part), 'col')]
    dot_general x20 -> x0, matrix products: 183 us -> none  [the longest x10 138 us: one_level(): jnp.dot(near_shift, loc_weight * coefs, precision=lax.Precision.HIGHEST)]
    psum x2 -> x0, waiting for transfers between devices: 79.2 us -> none  [shards(): obs_prior = lax.psum(partial_value, 'lev')]
    pallas_call x0 -> x1, Pallas kernels: none -> 60.1 us  [shards(): pl.pallas_call(kernel, name='window', out_shape=jax.ShapeDtypeStruct((LEV...]
    gather x4 -> x0, local copies, waits for them, and re-layouts: 26.3 us -> none  [the longest x2 13.4 us: shards(): picked = jnp.take(current, stencil, axis=2)]
    unnamed x3 -> x0, other arithmetic: 18 us -> none
    reduce_sum x9 -> x0, other arithmetic: 7.55 us -> none  [the longest x2 2.37 us: shards(): expected_part = jnp.sum(in_use * (prior_var + noise))]
    ppermute x4 -> x0, starting transfers between devices: 6.64 us -> none  [the longest x2 6.47 us: with_halo(): lax.ppermute(lax.slice_in_dim(block, 0, width, axis=dim), axis, backward)]
  transfers between devices with their start and end apart: 6 -> 0, of which waited for: 4 -> 0; matrix products, arithmetic and copies ran while one was open for 3% -> 0% of each run, Pallas kernels for 0% -> 0%
where the time goes in v1:
time: 65.8 us; the launch traced here: 65.6 us
  Pallas kernels  60.1 us (91%)
  local copies, waits for them, and re-layouts  5.42 us (8%)
    pallas_call x1, Pallas kernels, shards(): pl.pallas_call(kernel, name='window', out_shape=jax.ShapeDtypeStruct((LEV...  60.1 us
    unnamed x3, local copies, waits for them, and re-layouts  5.42 us

profile of v1, /device:TPU:1, one launch (start us, length us, event | category | flops | bytes accessed | tf_op | source)
XLA Modules:
  0.0 65.6 jit_solution(1030367298146235438)
XLA Ops:
  0.0 1.3 %copy.8.obs_count = s32[2,1]{1,0:T(2,128)} copy(s32[2,1]{0,1:T(1,128)} %param.9) | data formatting | bytes 16 | tf_op args[2]
  1.3 1.3 %copy.9.vw = f32[2,5,384]{2,1,0:T(8,128)} copy(f32[2,5,384]{2,0,1:T(2,128)} %param.13) | data formatting | bytes 30720 | tf_op args[6]
  2.6 60.1 %window.1 = f32[5,80,1024]{2,1,0:T(8,128)} custom-call(f32[5,80,1024]{2,1,0:T(8,128)} %state.1, s32[2,24576]{1,0:T(2,128)} %obs_col.1, s32[2,1]{1,0:T(2,128)} %copy.8.obs_count, f32[2,384]{1,0:T(2,128)} %obs_value.1, f32[2,384]{1,0:T(2,128)} %obs_var.1, f32[2,4,384]{2,1,0:T(4,128)} %hw.1, f32[2,5,384]{2,1,0:T(8,128)} %copy.9.vw), custom_call_target="tpu_custom_call" | custom-call | tf_op jit(solution)/shard_map/window/pallas_call | solution.py:342
  62.8 2.8 %copy.11 = f32[5,80,1024]{2,1,0:T(8,128)} copy(f32[5,80,1024]{2,1,0:T(8,128)} %window.1) | data formatting | bytes 3276800

commit v2 on v1

--- a/solution.py
+++ b/solution.py
@@ -51,14 +51,14 @@
     )
 
 
-def taper(dist):
-    r = dist * (1.0 / 256.0)
-    near = (((-0.25 * r + 0.5) * r + 0.625) * r - 5.0 / 3.0) * (r * r) + 1.0
-    t = jnp.maximum(2.0 - r, 0.0)
+def taper(d):
+    u = 1.0 / 256.0
+    near = ((-0.25 * u**5) * d + 0.5 * u**4) * d + 0.625 * u**3
+    near = (near * d - (5.0 / 3.0) * u**2) * (d * d) + 1.0
+    t = jnp.maximum(512.0 - d, 0.0)
     t2 = t * t
-    rs = jnp.maximum(r, 1.0)
-    far = (t2 * t2) * ((rs + 2.0) * rs - 0.5) * pl.reciprocal(12.0 * rs)
-    return jnp.where(r <= 1.0, near, far)
+    far = (t2 * t2) * ((u**5 / 12.0) * d + u**4 / 6.0 - (u**3 / 24.0) * pl.reciprocal(d))
+    return jnp.where(d <= 256.0, near, far)
 
 
 def remote(src, dst, send, recv, dev):
@@ -69,9 +69,9 @@
 
 
 def kernel(
-    state, obs_col, obs_count, obs_value, obs_var, hw, vw, out,
-    X, CEN, SPC, XHL, HH, HL, LOC, PT, RT, SC, ZH, ZL, MV, META, PART, RSB, PRI, G1, G2,
-    dma_sem, meta_s, meta_r, rs_s, rs_r, ag_s, ag_r, ha_s, ha_r, g1_s, g1_r, g2_s, g2_r,
+    state, obs_col, obs_count, obs_value, obs_var, hw_in, vw_in, out,
+    OCOL, OCNT, OVAL, OVAR, hw, vw, OUT, X, CEN, SPC, XHL, HH, HL, LOC, PT, RT, SC, ZH, ZL, MV, META, PART, RSB, PRI, G1, G2,
+    in_sem, out_sem, meta_s, meta_r, rs_s, rs_r, ag_s, ag_r, ha_s, ha_r, g1_s, g1_r, g2_s, g2_r,
 ):
     i = lax.axis_index("col")
     j = lax.axis_index("lev")
@@ -83,27 +83,39 @@
     lev_peers = [lax.rem(j + d, NLEV) for d in range(NLEV)]
     g1_peers = [
         {"col": lax.rem(y + dy, NY) * 16 + z * 2 + core, "lev": lax.rem(j + dl, NLEV)}
-        for dl in range(NLEV) for dy in range(NY) if dl or dy
+        for dl in (2, 1, 3, 0) for dy in (2, 1, 3, 0) if dl or dy
     ]
     g2_peers = [
         {"col": y * 16 + lax.rem(z + dz, NZ) * 2 + lax.rem(core + dc, 2), "lev": j}
-        for dz in range(NZ) for dc in range(2) if dz or dc
+        for dz in (4, 3, 5, 2, 6, 1, 7, 0) for dc in (1, 0) if dz or dc
     ]
     g1_me = j * NY + y
     g2_me = z * 2 + core
 
+    blocks = (i, left, right)
+    loads = [
+        pltpu.make_async_copy(obs_col.at[:, pl.ds(pl.multiple_of(b * CAP, CAP), CAP)], OCOL.at[n], in_sem.at[n])
+        for n, b in enumerate(blocks)
+    ]
+    for n, (src, dst) in enumerate(
+        ((obs_count, OCNT), (obs_value, OVAL), (obs_var, OVAR), (hw_in, hw), (vw_in, vw))
+    ):
+        loads.append(pltpu.make_async_copy(src, dst, in_sem.at[3 + n]))
+    load_state = pltpu.make_async_copy(state, X, in_sem.at[8])
+    for c in loads + [load_state]:
+        c.start()
     barrier = pltpu.get_barrier_semaphore()
     partners = g1_peers + g2_peers + [{"col": left, "lev": j}, {"col": right, "lev": j}]
     for dev in partners:
         pl.semaphore_signal(barrier, inc=1, device_id=dev, device_id_type=MESH)
-    load = pltpu.make_async_copy(state, X, dma_sem)
-    load.start()
-
-    starts = [obs_col[:, pl.ds(pl.multiple_of(b * CAP, CAP), CAP)] for b in (i, left, right)]
+    for c in loads:
+        c.wait()
+
+    starts = [OCOL[n] for n in range(3)]
     lane384 = lax.broadcasted_iota(jnp.int32, (1, CAP), 1)
-    use = [(lane384 < obs_count[b, 0]).astype(F32) for b in range(BATCHES)]
+    use = [(lane384 < OCNT[0:1, b : b + 1]).astype(F32) for b in range(BATCHES)]
     META[0] = jnp.concatenate(
-        [obs_value[...], obs_var[...], use[0], use[1], jnp.zeros((2, CAP), F32)], axis=0
+        [OVAL[...], OVAR[...], use[0], use[1], jnp.zeros((2, CAP), F32)], axis=0
     )
     MV[...] = jnp.stack(pad_quarters(META[0]))
     rel = [
@@ -130,17 +142,16 @@
                 m = jnp.where(t == n, w[n : n + 1], m)
             HH[b, rows, :], HL[b, rows, :] = split(m)
 
-    def build_taper(b):
+    def build_taper(b, grp):
         for half in range(2):
-            for grp in range(2):
-                blk = 0 if grp == 0 else 1 + half
-
-                @pl.loop(0, CAP // 32)
-                def _(k):
-                    rows = pl.ds(pl.multiple_of(k * 32, 32), 32)
-                    p = PT[rows, 2 * blk + b : 2 * blk + b + 1]
-                    c = (lax.broadcasted_iota(jnp.int32, (32, HALF), 1) + half * HALF).astype(F32)
-                    LOC[b, half, grp, rows, :] = taper(jnp.abs(p - c))
+            blk = 0 if grp == 0 else 1 + half
+
+            @pl.loop(0, CAP // 192)
+            def _(k):
+                rows = pl.ds(pl.multiple_of(k * 192, 192), 192)
+                p = PT[rows, 2 * blk + b : 2 * blk + b + 1]
+                c = (lax.broadcasted_iota(jnp.int32, (192, HALF), 1) + half * HALF).astype(F32)
+                LOC[half, grp, rows, :] = taper(jnp.abs(p - c))
 
     def partial_priors(b):
         @pl.loop(0, LEV)
@@ -150,7 +161,7 @@
             XHL[pl.ds(pl.multiple_of(l * MEM, MEM), MEM), :] = hi
             XHL[pl.ds(pl.multiple_of(LEV * MEM + l * MEM, MEM), MEM), :] = lo
 
-        v4 = pad_quarters(vw[b])
+        v4 = pad_quarters(vw[:, b, :])
         for n in range(2):
             cols = slice(n * 256, n * 256 + 256)
             a = jnp.dot(XHL[...], HH[b, :, cols], preferred_element_type=F32)
@@ -183,7 +194,7 @@
         return mean, dev, var
 
     build_gather(0)
-    load.wait()
+    load_state.wait()
     partial_priors(0)
     pl.semaphore_wait(barrier, len(partners))
 
@@ -191,7 +202,7 @@
         remote(META.at[0], META.at[1], meta_s.at[0], meta_r.at[0], {"col": right, "lev": j}),
         remote(META.at[0], META.at[2], meta_s.at[1], meta_r.at[1], {"col": left, "lev": j}),
     ]
-    pending = []
+    pending, stores = [], []
 
     for b in range(BATCHES):
         copies = []
@@ -203,32 +214,13 @@
         if b == 0:
             for c in meta_copies:
                 c.start()
-            build_taper(0)
+        build_taper(b, 0)
         prepare_spread()
         for c in copies:
             c.wait_recv()
         pending += copies
         prior = PART[b, j] + (RSB[b, 0] + RSB[b, 1] + RSB[b, 2])
         PRI[b, 0, j] = prior
-
-        def forward(q):
-            made = [
-                remote(PRI.at[b, 0, q], PRI.at[b, 1, q], ha_s.at[b, 0, q], ha_r.at[b, 0, q],
-                       {"col": right, "lev": j}),
-                remote(PRI.at[b, 0, q], PRI.at[b, 2, q], ha_s.at[b, 1, q], ha_r.at[b, 1, q],
-                       {"col": left, "lev": j}),
-            ]
-            for c in made:
-                c.start()
-            pending.extend(made)
-
-        gathers = []
-        for d in (2, 1, 3):
-            c = remote(PRI.at[b, 0, j], PRI.at[b, 0, j], ag_s.at[b, d - 1], ag_r.at[b, d - 1],
-                       {"col": i, "lev": lev_peers[d]})
-            c.start()
-            gathers.append((d, c))
-        forward(j)
 
         mean, dev, var = stats(prior)
         lane = lax.broadcasted_iota(jnp.int32, (1, LANES), 1)
@@ -242,8 +234,25 @@
         for dev_id in g1_peers:
             row = G1.at[b, pl.ds(g1_me, 1)]
             remote(row, row, g1_s.at[b], g1_r.at[b], dev_id).start()
-        if b == 0:
-            build_gather(1)
+        def forward(q):
+            made = [
+                remote(PRI.at[b, 0, q], PRI.at[b, 1, q], ha_s.at[b, 0, q], ha_r.at[b, 0, q],
+                       {"col": right, "lev": j}),
+                remote(PRI.at[b, 0, q], PRI.at[b, 2, q], ha_s.at[b, 1, q], ha_r.at[b, 1, q],
+                       {"col": left, "lev": j}),
+            ]
+            for c in made:
+                c.start()
+            pending.extend(made)
+
+        gathers = []
+        for d in (2, 1, 3):
+            c = remote(PRI.at[b, 0, j], PRI.at[b, 0, j], ag_s.at[b, d - 1], ag_r.at[b, d - 1],
+                       {"col": i, "lev": lev_peers[d]})
+            c.start()
+            gathers.append((d, c))
+        forward(j)
+        build_taper(b, 1)
         for d, c in gathers:
             c.wait_recv()
             forward(lax.rem(j + NLEV - d, NLEV))
@@ -274,14 +283,13 @@
                 RT[blk, cut, :] = tall.T.astype(BF16)
 
         def first_product(grp):
-            @pl.loop(0, LEV)
-            def _(l):
+            for l in range(LEV):
                 for c4 in range(4):
                     half, ct = c4 // 2, c4 % 2
                     blk = 0 if grp == 0 else 1 + half
                     cols = slice(c4 * 256, c4 * 256 + 256)
                     coef = jnp.dot(RT[blk], SPC[l, :, cols], preferred_element_type=F32)
-                    hi, lo = split(coef * LOC[b, half, grp, :, ct * 256 : ct * 256 + 256])
+                    hi, lo = split(coef * LOC[half, grp, :, ct * 256 : ct * 256 + 256])
                     ZH[l, grp * CAP : (grp + 1) * CAP, cols] = hi
                     ZL[l, grp * CAP : (grp + 1) * CAP, cols] = lo
 
@@ -290,7 +298,7 @@
         if b == 0:
             for c in meta_copies:
                 c.wait()
-            build_taper(1)
+            build_gather(1)
         for side in range(2):
             for q in range(4):
                 remote(PRI.at[b, 0, q], PRI.at[b, 1 + side, q], ha_s.at[b, side, q], ha_r.at[b, side, q],
@@ -316,10 +324,9 @@
                 SC[half, 0:MEM, cut] = hi
                 SC[half, MEM : 2 * MEM, cut] = lo
 
-        target = X if b + 1 < BATCHES else out
-
-        @pl.loop(0, LEV)
-        def _(l):
+        target = X if b + 1 < BATCHES else OUT
+
+        for l in range(LEV):
             for c4 in range(4):
                 half = c4 // 2
                 cols = slice(c4 * 256, c4 * 256 + 256)
@@ -328,31 +335,55 @@
                 centre = CEN[l, 0:1, cols]
                 base = centre + root * (X[l, :, cols] - centre)
                 target[l, :, cols] = base + (a[:MEM] + a[MEM:] + r)
+            if b + 1 == BATCHES:
+                c = pltpu.make_async_copy(OUT.at[l], out.at[l], out_sem.at[l])
+                c.start()
+                stores.append(c)
 
         if b + 1 < BATCHES:
             partial_priors(b + 1)
 
+    for c in stores:
+        c.wait()
     for c in pending:
         c.wait_send()
 
 
+def hand_over(src, dst, buf, in_sem, out_sem):
+    ins = [pltpu.make_async_copy(src.at[l], buf.at[l], in_sem.at[l]) for l in range(LEV)]
+    outs = [pltpu.make_async_copy(buf.at[l], dst.at[l], out_sem.at[l]) for l in range(LEV)]
+    for c in ins:
+        c.start()
+    for c, o in zip(ins, outs):
+        c.wait()
+        o.start()
+    for o in outs:
+        o.wait()
+
+
 def shards(state, obs_col, obs_count, obs_value, obs_var, horiz_weight, vert_weight):
-    vm = pl.BlockSpec(memory_space=pltpu.VMEM)
     dma = pltpu.SemaphoreType.DMA
-    return pl.pallas_call(
+    result = pl.pallas_call(
         kernel,
         name="window",
         out_shape=jax.ShapeDtypeStruct((LEV, MEM, COLS), F32),
-        in_specs=[pl.BlockSpec(memory_space=pl.ANY), vm, pl.BlockSpec(memory_space=pltpu.SMEM), vm, vm, vm, vm],
-        out_specs=vm,
+        in_specs=[pl.BlockSpec(memory_space=pltpu.HBM)] * 7,
+        out_specs=pl.BlockSpec(memory_space=pl.ANY),
         scratch_shapes=[
+            pltpu.VMEM((3, BATCHES, CAP), jnp.int32),
+            pltpu.VMEM((1, BATCHES), jnp.int32),
+            pltpu.VMEM((BATCHES, CAP), F32),
+            pltpu.VMEM((BATCHES, CAP), F32),
+            pltpu.VMEM((BATCHES, 4, CAP), F32),
+            pltpu.VMEM((LEV, BATCHES, CAP), F32),
+            pltpu.VMEM((LEV, MEM, COLS), F32),
             pltpu.VMEM((LEV, MEM, COLS), F32),
             pltpu.VMEM((LEV, 8, COLS), F32),
             pltpu.VMEM((LEV, 256, COLS), BF16),
             pltpu.VMEM((2 * LEV * MEM, COLS), BF16),
             pltpu.VMEM((BATCHES, COLS, 4 * LANES), BF16),
             pltpu.VMEM((BATCHES, COLS, 4 * LANES), BF16),
-            pltpu.VMEM((BATCHES, 2, 2, CAP, HALF), F32),
+            pltpu.VMEM((2, 2, CAP, HALF), F32),
             pltpu.VMEM((CAP, LANES), F32),
             pltpu.VMEM((3, CAP, 256), BF16),
             pltpu.VMEM((2, 2 * MEM, 2 * CAP), BF16),
@@ -365,7 +396,8 @@
             pltpu.VMEM((BATCHES, 3, 4, MEM, LANES), F32),
             pltpu.VMEM((BATCHES, 16, LANES), F32),
             pltpu.VMEM((BATCHES, 16, LANES), F32),
-            dma,
+            dma((9,)),
+            dma((LEV,)),
             dma((2,)), dma((2,)),
             dma((BATCHES, 3)), dma((BATCHES, 3)),
             dma((BATCHES, 3)), dma((BATCHES, 3)),
@@ -376,7 +408,18 @@
         compiler_params=pltpu.CompilerParams(
             collective_id=0, has_side_effects=True, vmem_limit_bytes=56 * 1024 * 1024
         ),
-    )(state, obs_col, obs_count, obs_value, obs_var, horiz_weight, vert_weight)
+    )(
+        state, obs_col, obs_count.T, obs_value, obs_var, horiz_weight, jnp.transpose(vert_weight, (1, 0, 2))
+    )
+    return pl.pallas_call(
+        hand_over,
+        name="hand_over",
+        out_shape=jax.ShapeDtypeStruct((LEV, MEM, COLS), F32),
+        in_specs=[pl.BlockSpec(memory_space=pl.ANY)],
+        out_specs=pl.BlockSpec(memory_space=pl.ANY),
+        scratch_shapes=[pltpu.VMEM((LEV, MEM, COLS), F32), dma((LEV,)), dma((LEV,))],
+        compiler_params=pltpu.CompilerParams(vmem_limit_bytes=56 * 1024 * 1024),
+    )(result)
 
 
 def solution(mesh):

time: 65.8 us -> 49.8 us (0.76)
  Pallas kernels: 60.1 us -> 49.5 us
  local copies, waits for them, and re-layouts: 5.42 us -> 0 us
    pallas_call x1, Pallas kernels: 60.1 us -> 47.3 us  [shards(): pl.pallas_call(kernel, name='window', out_shape=jax.ShapeDtypeStruct((LEV...]
    unnamed x3 -> x0, local copies, waits for them, and re-layouts: 5.42 us -> none
    pallas_call x0 -> x1, Pallas kernels: none -> 2.21 us  [shards(): pl.pallas_call(hand_over, name='hand_over', out_shape=jax.ShapeDtypeStruc...]
where the time goes in v2:
time: 49.8 us; the launch traced here: 49.6 us
  Pallas kernels  49.5 us (99%)
    pallas_call x1, Pallas kernels, shards(): pl.pallas_call(kernel, name='window', out_shape=jax.ShapeDtypeStruct((LEV...  47.3 us
    pallas_call x1, Pallas kernels, shards(): pl.pallas_call(hand_over, name='hand_over', out_shape=jax.ShapeDtypeStruc...  2.21 us

profile of v2, /device:TPU:1, one launch (start us, length us, event | category | flops | bytes accessed | tf_op | source)
XLA Modules:
  0.0 49.6 jit_solution(6110759819117449305)
XLA Ops:
  0.0 47.3 %window.1.src = f32[5,80,1024]{2,1,0:T(8,128)} custom-call(f32[5,80,1024]{2,1,0:T(8,128)} %state.1, s32[2,24576]{1,0:T(2,128)} %obs_col.1, s32[1,2]{1,0:T(1,128)} %bitcast.3, f32[2,384]{1,0:T(2,128)} %obs_value.1, f32[2,384]{1,0:T(2,128)} %obs_var.1, f32[2,4,384]{2,1,0:T(4,128)} %hw_in.1, f32[5,2,384]{2,1,0:T(2,128)} %bitcast.2), custom_call_target="tpu_custom_call" | custom-call | tf_op jit(solution)/shard_map/window/pallas_call | solution.py:366
  47.3 2.2 %hand_over.1 = f32[5,80,1024]{2,1,0:T(8,128)} custom-call(f32[5,80,1024]{2,1,0:T(8,128)} %window.1.src), custom_call_target="tpu_custom_call" | custom-call | tf_op jit(solution)/shard_map/hand_over/pallas_call | solution.py:414

commit v3 on v2

--- a/solution.py
+++ b/solution.py
@@ -16,6 +16,7 @@
 COLS = 1024
 CAP = 384
 QUART = 96
+FOLD = 64
 LANES = 128
 HALF = 512
 NZ = 8
@@ -49,6 +50,20 @@
         ],
         axis=1,
     )
+
+
+def fold(x):
+    lane = lax.broadcasted_iota(jnp.int32, (FOLD, LANES), 1)
+    last = x[FOLD:]
+    extra = [pltpu.roll(last, 96 - 32 * k, 1) for k in range(3)] + [jnp.zeros_like(last)]
+    return jnp.where(lane < QUART, x[:FOLD], jnp.concatenate(extra, axis=0))
+
+
+def unfold(p):
+    lane = lax.broadcasted_iota(jnp.int32, (MEM - FOLD, LANES), 1)
+    r = [pltpu.roll(p[16 * k : 16 * k + 16], 32 + 32 * k, 1) for k in range(3)]
+    last = jnp.where(lane < 32, r[0], jnp.where(lane < 64, r[1], r[2]))
+    return jnp.concatenate([p, last], axis=0)
 
 
 def taper(d):
@@ -114,17 +129,6 @@
     starts = [OCOL[n] for n in range(3)]
     lane384 = lax.broadcasted_iota(jnp.int32, (1, CAP), 1)
     use = [(lane384 < OCNT[0:1, b : b + 1]).astype(F32) for b in range(BATCHES)]
-    META[0] = jnp.concatenate(
-        [OVAL[...], OVAR[...], use[0], use[1], jnp.zeros((2, CAP), F32)], axis=0
-    )
-    MV[...] = jnp.stack(pad_quarters(META[0]))
-    rel = [
-        (starts[0] - i * COLS).astype(F32),
-        (starts[1] - left * COLS - COLS).astype(F32),
-        (starts[2] - right * COLS + COLS).astype(F32),
-    ]
-    PT[...] = jnp.concatenate(rel + [jnp.zeros((LANES - 6, CAP), F32)], axis=0).T
-
     def build_gather(b):
         lane = lax.broadcasted_iota(jnp.int32, (1, LANES), 1)
         valid = lane < QUART
@@ -153,14 +157,10 @@
                 c = (lax.broadcasted_iota(jnp.int32, (192, HALF), 1) + half * HALF).astype(F32)
                 LOC[half, grp, rows, :] = taper(jnp.abs(p - c))
 
+    def split_state(l, cols, x):
+        XHL[l * MEM : (l + 1) * MEM, cols], XHL[(LEV + l) * MEM : (LEV + l + 1) * MEM, cols] = split(x)
+
     def partial_priors(b):
-        @pl.loop(0, LEV)
-        def _(l):
-            x = X[l]
-            hi, lo = split(x)
-            XHL[pl.ds(pl.multiple_of(l * MEM, MEM), MEM), :] = hi
-            XHL[pl.ds(pl.multiple_of(LEV * MEM + l * MEM, MEM), MEM), :] = lo
-
         v4 = pad_quarters(vw[:, b, :])
         for n in range(2):
             cols = slice(n * 256, n * 256 + 256)
@@ -172,8 +172,8 @@
                 term = a[l * MEM : (l + 1) * MEM] + a[(LEV + l) * MEM : (LEV + l + 1) * MEM]
                 term = (term + r[l * MEM : (l + 1) * MEM]) * v[l : l + 1]
                 total = term if total is None else total + term
-            PART[b, 2 * n] = total[:, :LANES]
-            PART[b, 2 * n + 1] = total[:, LANES:]
+            PART[b, 2 * n] = fold(total[:, :LANES])
+            PART[b, 2 * n + 1] = fold(total[:, LANES:])
 
     def prepare_spread():
         @pl.loop(0, LEV)
@@ -195,6 +195,8 @@
 
     build_gather(0)
     load_state.wait()
+    for l in range(LEV):
+        split_state(l, slice(0, COLS), X[l])
     partial_priors(0)
     pl.semaphore_wait(barrier, len(partners))
 
@@ -212,6 +214,16 @@
             c.start()
             copies.append(c)
         if b == 0:
+            META[0] = jnp.concatenate(
+                [OVAL[...], OVAR[...], use[0], use[1], jnp.zeros((2, CAP), F32)], axis=0
+            )
+            MV[...] = jnp.stack(pad_quarters(META[0]))
+            rel = [
+                (starts[0] - i * COLS).astype(F32),
+                (starts[1] - left * COLS - COLS).astype(F32),
+                (starts[2] - right * COLS + COLS).astype(F32),
+            ]
+            PT[...] = jnp.concatenate(rel + [jnp.zeros((LANES - 6, CAP), F32)], axis=0).T
             for c in meta_copies:
                 c.start()
         build_taper(b, 0)
@@ -222,7 +234,7 @@
         prior = PART[b, j] + (RSB[b, 0] + RSB[b, 1] + RSB[b, 2])
         PRI[b, 0, j] = prior
 
-        mean, dev, var = stats(prior)
+        mean, dev, var = stats(unfold(prior))
         lane = lax.broadcasted_iota(jnp.int32, (1, LANES), 1)
         value = MV[j, b : b + 1]
         noise = MV[j, 2 + b : 3 + b]
@@ -246,13 +258,15 @@
             pending.extend(made)
 
         gathers = []
-        for d in (2, 1, 3):
+        for d in (1, 3, 2):
             c = remote(PRI.at[b, 0, j], PRI.at[b, 0, j], ag_s.at[b, d - 1], ag_r.at[b, d - 1],
                        {"col": i, "lev": lev_peers[d]})
             c.start()
             gathers.append((d, c))
         forward(j)
         build_taper(b, 1)
+        if b == 0:
+            build_gather(1)
         for d, c in gathers:
             c.wait_recv()
             forward(lax.rem(j + NLEV - d, NLEV))
@@ -268,7 +282,7 @@
         kept = []
 
         def regression(blk):
-            prior3 = pack_quarters(*[PRI[b, blk, q] for q in range(4)])
+            prior3 = pack_quarters(*[unfold(PRI[b, blk, q]) for q in range(4)])
             mean, dev, var = stats(prior3)
             used = META[blk, 4 + b : 5 + b]
             anom = dev * used
@@ -282,10 +296,12 @@
                 tall = jnp.concatenate([hi[:, cut], lo[:, cut], hi[:, cut], jnp.zeros((16, LANES), F32)], axis=0)
                 RT[blk, cut, :] = tall.T.astype(BF16)
 
-        def first_product(grp):
+        def first_product(grp, halves=(0, 1)):
             for l in range(LEV):
                 for c4 in range(4):
                     half, ct = c4 // 2, c4 % 2
+                    if half not in halves:
+                        continue
                     blk = 0 if grp == 0 else 1 + half
                     cols = slice(c4 * 256, c4 * 256 + 256)
                     coef = jnp.dot(RT[blk], SPC[l, :, cols], preferred_element_type=F32)
@@ -298,14 +314,12 @@
         if b == 0:
             for c in meta_copies:
                 c.wait()
-            build_gather(1)
         for side in range(2):
             for q in range(4):
                 remote(PRI.at[b, 0, q], PRI.at[b, 1 + side, q], ha_s.at[b, side, q], ha_r.at[b, side, q],
                        {"col": right, "lev": j}).wait_recv()
-        regression(1)
-        regression(2)
-        first_product(1)
+            regression(1 + side)
+            first_product(1, (side,))
 
         all15 = G2.at[b, pl.ds(0, 15)]
         remote(all15, all15, g2_s.at[b], g2_r.at[b], g2_peers[0]).wait()
@@ -334,7 +348,10 @@
                 r = jnp.dot(SC[half, 0:MEM], ZL[l, :, cols], preferred_element_type=F32)
                 centre = CEN[l, 0:1, cols]
                 base = centre + root * (X[l, :, cols] - centre)
-                target[l, :, cols] = base + (a[:MEM] + a[MEM:] + r)
+                new = base + (a[:MEM] + a[MEM:] + r)
+                target[l, :, cols] = new
+                if b + 1 < BATCHES:
+                    split_state(l, cols, new)
             if b + 1 == BATCHES:
                 c = pltpu.make_async_copy(OUT.at[l], out.at[l], out_sem.at[l])
                 c.start()
@@ -391,9 +408,9 @@
             pltpu.VMEM((LEV, 2 * CAP, COLS), BF16),
             pltpu.VMEM((4, 8, LANES), F32),
             pltpu.VMEM((3, 8, CAP), F32),
-            pltpu.VMEM((BATCHES, 4, MEM, LANES), F32),
-            pltpu.VMEM((BATCHES, 3, MEM, LANES), F32),
-            pltpu.VMEM((BATCHES, 3, 4, MEM, LANES), F32),
+            pltpu.VMEM((BATCHES, 4, FOLD, LANES), F32),
+            pltpu.VMEM((BATCHES, 3, FOLD, LANES), F32),
+            pltpu.VMEM((BATCHES, 3, 4, FOLD, LANES), F32),
             pltpu.VMEM((BATCHES, 16, LANES), F32),
             pltpu.VMEM((BATCHES, 16, LANES), F32),
             dma((9,)),

time: 49.8 us -> 47.8 us (0.960)
  Pallas kernels: 49.5 us -> 47.5 us
    pallas_call x1, Pallas kernels: 47.3 us -> 45.3 us  [shards(): pl.pallas_call(kernel, name='window', out_shape=jax.ShapeDtypeStruct((LEV...]
where the time goes in v3:
time: 47.8 us; the launch traced here: 47.7 us
  Pallas kernels  47.5 us (99%)
    pallas_call x1, Pallas kernels, shards(): pl.pallas_call(kernel, name='window', out_shape=jax.ShapeDtypeStruct((LEV...  45.3 us
    pallas_call x1, Pallas kernels, shards(): pl.pallas_call(hand_over, name='hand_over', out_shape=jax.ShapeDtypeStruc...  2.21 us

profile of v3, /device:TPU:1, one launch (start us, length us, event | category | flops | bytes accessed | tf_op | source)
XLA Modules:
  0.0 47.7 jit_solution(5892189621478119557)
XLA Ops:
  0.0 45.3 %window.1.src = f32[5,80,1024]{2,1,0:T(8,128)} custom-call(f32[5,80,1024]{2,1,0:T(8,128)} %state.1, s32[2,24576]{1,0:T(2,128)} %obs_col.1, s32[1,2]{1,0:T(1,128)} %bitcast.3, f32[2,384]{1,0:T(2,128)} %obs_value.1, f32[2,384]{1,0:T(2,128)} %obs_var.1, f32[2,4,384]{2,1,0:T(4,128)} %hw_in.1, f32[5,2,384]{2,1,0:T(2,128)} %bitcast.2), custom_call_target="tpu_custom_call" | custom-call | tf_op jit(solution)/shard_map/window/pallas_call | solution.py:383
  45.3 2.2 %hand_over.1 = f32[5,80,1024]{2,1,0:T(8,128)} custom-call(f32[5,80,1024]{2,1,0:T(8,128)} %window.1.src), custom_call_target="tpu_custom_call" | custom-call | tf_op jit(solution)/shard_map/hand_over/pallas_call | solution.py:431

commit v4 on v3

--- a/solution.py
+++ b/solution.py
@@ -247,11 +247,13 @@
             row = G1.at[b, pl.ds(g1_me, 1)]
             remote(row, row, g1_s.at[b], g1_r.at[b], dev_id).start()
         def forward(q):
+            off = lax.rem(i + 63 + 2 * core, 64)
+            on = i + 1 - 2 * core
             made = [
-                remote(PRI.at[b, 0, q], PRI.at[b, 1, q], ha_s.at[b, 0, q], ha_r.at[b, 0, q],
-                       {"col": right, "lev": j}),
-                remote(PRI.at[b, 0, q], PRI.at[b, 2, q], ha_s.at[b, 1, q], ha_r.at[b, 1, q],
-                       {"col": left, "lev": j}),
+                remote(PRI.at[b, 0, q], PRI.at[b, 2 - core, q], ha_s.at[b, 1 - core, q], ha_r.at[b, 1 - core, q],
+                       {"col": off, "lev": j}),
+                remote(PRI.at[b, 0, q], PRI.at[b, 1 + core, q], ha_s.at[b, core, q], ha_r.at[b, core, q],
+                       {"col": on, "lev": j}),
             ]
             for c in made:
                 c.start()
@@ -287,7 +289,7 @@
             used = META[blk, 4 + b : 5 + b]
             anom = dev * used
             innov = (META[blk, b : b + 1] - mean) * used
-            kept.append((anom, innov, var))
+            kept.append((blk, anom, innov, var))
             regress = anom / ((MEM - 1) * (var + EPS))
             hi = regress.astype(BF16).astype(F32)
             lo = regress - hi
@@ -296,45 +298,50 @@
                 tall = jnp.concatenate([hi[:, cut], lo[:, cut], hi[:, cut], jnp.zeros((16, LANES), F32)], axis=0)
                 RT[blk, cut, :] = tall.T.astype(BF16)
 
-        def first_product(grp, halves=(0, 1)):
+        def own_product():
             for l in range(LEV):
                 for c4 in range(4):
                     half, ct = c4 // 2, c4 % 2
-                    if half not in halves:
-                        continue
-                    blk = 0 if grp == 0 else 1 + half
                     cols = slice(c4 * 256, c4 * 256 + 256)
-                    coef = jnp.dot(RT[blk], SPC[l, :, cols], preferred_element_type=F32)
-                    hi, lo = split(coef * LOC[half, grp, :, ct * 256 : ct * 256 + 256])
-                    ZH[l, grp * CAP : (grp + 1) * CAP, cols] = hi
-                    ZL[l, grp * CAP : (grp + 1) * CAP, cols] = lo
+                    coef = jnp.dot(RT[0], SPC[l, :, cols], preferred_element_type=F32)
+                    hi, lo = split(coef * LOC[half, 0, :, ct * 256 : ct * 256 + 256])
+                    ZH[l, 0:CAP, cols] = hi
+                    ZL[l, 0:CAP, cols] = lo
+
+        def side_product(side):
+            for l in range(LEV):
+                for ct in range(2):
+                    cols = pl.ds(pl.multiple_of(side * HALF + ct * 256, 256), 256)
+                    coef = jnp.dot(RT[1 + side], SPC[l, :, cols], preferred_element_type=F32)
+                    hi, lo = split(coef * LOC[side, 1, :, ct * 256 : ct * 256 + 256])
+                    ZH[l, CAP : 2 * CAP, cols] = hi
+                    ZL[l, CAP : 2 * CAP, cols] = lo
 
         regression(0)
-        first_product(0)
+        own_product()
         if b == 0:
             for c in meta_copies:
                 c.wait()
-        for side in range(2):
+        for side in (1 - core, core):
             for q in range(4):
                 remote(PRI.at[b, 0, q], PRI.at[b, 1 + side, q], ha_s.at[b, side, q], ha_r.at[b, side, q],
                        {"col": right, "lev": j}).wait_recv()
             regression(1 + side)
-            first_product(1, (side,))
+            side_product(side)
 
         all15 = G2.at[b, pl.ds(0, 15)]
         remote(all15, all15, g2_s.at[b], g2_r.at[b], g2_peers[0]).wait()
         sums = jnp.sum(G2[b], axis=0, keepdims=True)
         inflation = sums[:, 0:1] / sums[:, 64:65]
         root = jnp.sqrt(inflation)
-        for blk in range(3):
-            anom, innov, var = kept[blk]
+        for n, (blk, anom, innov, var) in enumerate(kept):
             noise = META[blk, 2 + b : 3 + b]
             v = inflation * var
             tot = v + noise
             shift = v * innov / tot + ((jnp.sqrt(noise / tot) - 1.0) * root) * anom
             hi, lo = split(shift)
-            cut = slice(0, CAP) if blk == 0 else slice(CAP, 2 * CAP)
-            for half in ((0, 1) if blk == 0 else (blk - 1,)):
+            cut = slice(0, CAP) if n == 0 else slice(CAP, 2 * CAP)
+            for half in (0, 1) if n == 0 else (blk - 1,):
                 SC[half, 0:MEM, cut] = hi
                 SC[half, MEM : 2 * MEM, cut] = lo
 

time: 47.8 us -> 47.9 us (level)
  no operation moved by 1% of the time
where the time goes in v4:
time: 47.9 us; the launch traced here: 47.7 us
  Pallas kernels  47.6 us (99%)
    pallas_call x1, Pallas kernels, shards(): pl.pallas_call(kernel, name='window', out_shape=jax.ShapeDtypeStruct((LEV...  45.4 us
    pallas_call x1, Pallas kernels, shards(): pl.pallas_call(hand_over, name='hand_over', out_shape=jax.ShapeDtypeStruc...  2.21 us

profile of v4, /device:TPU:1, one launch (start us, length us, event | category | flops | bytes accessed | tf_op | source)
XLA Modules:
  0.0 47.7 jit_solution(1612677195660376154)
XLA Ops:
  0.0 45.4 %window.1.src = f32[5,80,1024]{2,1,0:T(8,128)} custom-call(f32[5,80,1024]{2,1,0:T(8,128)} %state.1, s32[2,24576]{1,0:T(2,128)} %obs_col.1, s32[1,2]{1,0:T(1,128)} %bitcast.3, f32[2,384]{1,0:T(2,128)} %obs_value.1, f32[2,384]{1,0:T(2,128)} %obs_var.1, f32[2,4,384]{2,1,0:T(4,128)} %hw_in.1, f32[5,2,384]{2,1,0:T(2,128)} %bitcast.2), custom_call_target="tpu_custom_call" | custom-call | tf_op jit(solution)/shard_map/window/pallas_call | solution.py:390
  45.4 2.2 %hand_over.1 = f32[5,80,1024]{2,1,0:T(8,128)} custom-call(f32[5,80,1024]{2,1,0:T(8,128)} %window.1.src), custom_call_target="tpu_custom_call" | custom-call | tf_op jit(solution)/shard_map/hand_over/pallas_call | solution.py:438
